TPU v7x, 32 devices: a whole 2x2x4 slice. The times are simulated.
32 devices in a mesh: cp: 8 (over z, x), dp: 4 (over y, core).
Axes of the slice: x: 2, y: 2, z: 4, core: 2. Of those that a mesh axis runs over, the one named last changes fastest.
Arguments:
- queries: bfloat16 [4, 1024, 2560], P('dp', 'cp'), may hold values from -6 to 6
- keys: bfloat16 [4, 1024, 2560], P('dp', 'cp'), may hold values from -6 to 6
- values: bfloat16 [4, 1024, 2560], P('dp', 'cp'), may hold values from -6 to 6
- outputs: bfloat16 [4, 1024, 2560], P('dp', 'cp'), may hold values from -6 to 6
- d_out: bfloat16 [4, 1024, 2560], P('dp', 'cp'), may hold values from -6 to 6
- log_norm: float32 [4, 1024, 20], P('dp', 'cp'), may hold values from 3 to 7
- lengths: int32 [4, 3], P('dp'), may hold values from 1 to 4, as said below
- fire_w1: float32 [32], replicated, may hold values from -6 to 6
- fire_b1: float32 [32], replicated, may hold values from -3 to 3
- fire_w2: float32 [32, 20], replicated, may hold values from -1 to 1
Outputs:
- grad_queries: bfloat16 [4, 1024, 2560], P('dp', 'cp')
- grad_keys: bfloat16 [4, 1024, 2560], P('dp', 'cp')
- grad_values: bfloat16 [4, 1024, 2560], P('dp', 'cp')
- grad_w1: float32 [32], replicated
- grad_b1: float32 [32], replicated
- grad_w2: float32 [32, 20], replicated
Inputs may be any that keep to these rules, and one draw needn't show every extreme that they name: `lengths`: each batch row's 3 sequences fill its 8 blocks in order, each a whole number of blocks; the first sequence of every row takes exactly 4 blocks.
All inputs are finite; a program needn't handle non-finite values.
Results may differ from a plain program's by a relative error of at most 0.0054.
Values may be sent and summed in bfloat16 or wider, within the bound.
A program may use at most 128 MiB of HBM per device.

v0:
```python
import jax
import jax.numpy as jnp
from jax import lax
from jax.sharding import PartitionSpec as P

GROUP_MOST = 4


fire_floor = 64.0


def shifted_2(block, axis, distance):
    devices = range(lax.axis_size(axis))
    route = [(i - distance, i) for i in devices if i - distance in devices]
    return lax.ppermute(block, axis, route)


def shifted_3(shard, axis, by):
    count = lax.axis_size(axis)
    return lax.ppermute(shard, axis, [(i, (i + by) % count) for i in range(count)])


def seat_of(length_row, device):
    ends = jnp.cumsum(length_row)
    sequence = jnp.sum((ends <= device).astype(jnp.int32))
    before = jnp.sum(
        jnp.where(jnp.arange(length_row.shape[0], dtype=jnp.int32) < sequence, length_row, 0)
    )
    return (sequence, device - before)


def pair_terms(
    query_heads,
    grad_heads,
    log_block,
    delta_block,
    key_heads,
    value_heads,
    query_seq,
    query_pos,
    key_seq,
    key_pos,
    fire_w1,
    fire_b1,
    fire_w2,
):
    highest = lax.Precision.HIGHEST
    scale_value = query_heads.shape[2] ** (-0.5)
    allowed = (query_seq == key_seq) & (key_pos[None, :] <= query_pos[:, None])
    distance = jnp.maximum(query_pos[:, None] - key_pos[None, :], 0).astype(jnp.float32)
    denom = jnp.log1p(jnp.maximum(query_pos.astype(jnp.float32), fire_floor))
    ratio = jnp.log1p(distance) / denom[:, None]
    hidden_pre = fire_w1[:, None, None] * ratio[None] + fire_b1[:, None, None]
    hidden_act = jnp.maximum(hidden_pre, 0.0)
    pair_bias = jnp.einsum("cqk,ch->hqk", hidden_act, fire_w2, precision=highest)
    scores = (
        jnp.einsum("qhd,khd->hqk", query_heads, key_heads, preferred_element_type=jnp.float32)
        * scale_value
        + pair_bias
    )
    shifted = jnp.where(allowed[None], scores - log_block.T[:, :, None], -1e30)
    prob_block = jnp.exp(shifted)
    dprob = jnp.einsum("qhd,khd->hqk", grad_heads, value_heads, preferred_element_type=jnp.float32)
    dscore = prob_block * (dprob - delta_block.T[:, :, None])
    prob_low = prob_block.astype(jnp.bfloat16)
    score_low = dscore.astype(jnp.bfloat16)
    grad_query = (
        jnp.einsum("hqk,khd->qhd", score_low, key_heads, preferred_element_type=jnp.float32)
        * scale_value
    )
    grad_key = (
        jnp.einsum("hqk,qhd->khd", score_low, query_heads, preferred_element_type=jnp.float32)
        * scale_value
    )
    grad_value = jnp.einsum(
        "hqk,qhd->khd", prob_low, grad_heads, preferred_element_type=jnp.float32
    )
    grad_second = jnp.einsum("hqk,cqk->ch", dscore, hidden_act, precision=highest)
    grad_act = jnp.einsum("hqk,ch->cqk", dscore, fire_w2, precision=highest)
    grad_pre = jnp.where(hidden_pre > 0, grad_act, 0.0)
    grad_first = jnp.sum(grad_pre * ratio[None], axis=(1, 2))
    grad_bias = jnp.sum(grad_pre, axis=(1, 2))
    return (grad_query, grad_key, grad_value, grad_first, grad_bias, grad_second)


def rotate_keys(key_value):
    return shifted_2(key_value, "cp", 1)


def on_device(queries, keys, values, outputs, d_out, log_norm, lengths, fire_w1, fire_b1, fire_w2):
    rows_dev = queries.shape[1]
    heads_count = log_norm.shape[2]
    feature_count = queries.shape[2]
    head_size = feature_count // heads_count
    cp_count = lax.axis_size("cp")
    my_index = lax.axis_index("cp")
    length_row = lengths[0]
    reach = GROUP_MOST - 1
    query_heads = queries[0].reshape(rows_dev, heads_count, head_size)
    key_heads = keys[0].reshape(rows_dev, heads_count, head_size)
    value_heads = values[0].reshape(rows_dev, heads_count, head_size)
    grad_heads = d_out[0].reshape(rows_dev, heads_count, head_size)
    out_heads = outputs[0].reshape(rows_dev, heads_count, head_size)
    log_block = log_norm[0]
    delta_block = jnp.einsum(
        "qhd,qhd->qh", grad_heads, out_heads, preferred_element_type=jnp.float32
    )
    token_index = jnp.arange(rows_dev, dtype=jnp.int32)

    def seat_positions(device):
        sequence, offset = seat_of(length_row, device)
        return (sequence, offset * rows_dev + token_index)

    my_seq, my_pos = seat_positions(my_index)
    local = pair_terms(
        query_heads,
        grad_heads,
        log_block,
        delta_block,
        key_heads,
        value_heads,
        my_seq,
        my_pos,
        my_seq,
        my_pos,
        fire_w1,
        fire_b1,
        fire_w2,
    )
    key_value = jnp.stack([key_heads, value_heads])

    def carried_hop(hop_index, carry):
        moving_kv, moving_grads, grad_q, first, bias_sum, second = carry
        moving_kv = rotate_keys(moving_kv)
        moving_grads = shifted_3(moving_grads, "cp", 1)
        key_seq, key_pos = seat_positions((my_index - hop_index) % cp_count)
        terms = pair_terms(
            query_heads,
            grad_heads,
            log_block,
            delta_block,
            moving_kv[0],
            moving_kv[1],
            my_seq,
            my_pos,
            key_seq,
            key_pos,
            fire_w1,
            fire_b1,
            fire_w2,
        )
        moving_grads = moving_grads + jnp.stack([terms[1], terms[2]])
        return (
            moving_kv,
            moving_grads,
            grad_q + terms[0],
            first + terms[3],
            bias_sum + terms[4],
            second + terms[5],
        )

    start = (key_value, jnp.stack([local[1], local[2]]), local[0], local[3], local[4], local[5])
    result = lax.fori_loop(1, GROUP_MOST, carried_hop, start)
    grad_q, first, bias_sum, second = (result[2], result[3], result[4], result[5])
    home_grads = shifted_3(result[1].astype(jnp.bfloat16), "cp", -reach).astype(jnp.float32)
    grad_k, grad_v = (home_grads[0], home_grads[1])
    first, bias_sum, second = lax.psum((first, bias_sum, second), ("cp", "dp"))
    factor = (lax.axis_size("dp") * cp_count * rows_dev) ** (-0.5)
    out_shape = (1, rows_dev, feature_count)
    return (
        grad_q.reshape(out_shape).astype(jnp.bfloat16),
        grad_k.reshape(out_shape).astype(jnp.bfloat16),
        grad_v.reshape(out_shape).astype(jnp.bfloat16),
        first * factor,
        bias_sum * factor,
        second * factor,
    )


def solution(mesh):
    placed = (
        P("dp", "cp", None),
        P("dp", "cp", None),
        P("dp", "cp", None),
        P("dp", "cp", None),
        P("dp", "cp", None),
        P("dp", "cp", None),
        P("dp", None),
        P(),
        P(),
        P(),
    )
    return jax.shard_map(
        on_device,
        mesh=mesh,
        in_specs=placed,
        out_specs=(P("dp", "cp", None), P("dp", "cp", None), P("dp", "cp", None), P(), P(), P()),
        check_vma=False,
    )
```

profile of v0, /device:TPU:0, one launch (start us, length us, event | category | flops | bytes accessed | tf_op | source)
XLA Modules:
  0.0 403.4 jit_solution(13713996151022838586)
XLA Ops:
  2.2 1.9 fusion.86
  5.7 1.5 copy.40
  7.2 1.1 copy.41
  9.4 1.1 copy.51
  11.1 1.3 fusion.66
  12.5 1.8 fusion.55
  15.1 1.7 convolution_bitcast_fusion.1
  17.5 3.3 fusion.90
  20.8 2.4 fusion.67
  23.2 1.7 fusion.59
  24.9 1.7 fusion.60
  26.6 1.2 pad_maximum_fusion.1
  27.8 2.5 copy.60
  30.3 3.1 pad_maximum_fusion
  33.4 275.6 %while.27 = (s32[]{:T(128)}, bf16[2,128,20,128]{3,1,2,0:T(8,128)(2,1)}, f32[2,128,20,128]{3,1,2,0:T(8,128)}, f32[128,20,128]{2,0,1:T(8,128)}, f32[32]{0:T(128)S(...) while((s32[]{:T(128)}, ...), condition=%wide.region_10.11_spmd.clone.clone, body=%wide.region_5.10_spmd.clone.clone.sunk | while | flops 809075968 | bytes 60236068 | solution.py:163
  33.4 4.9 %collective-permute-start = (bf16[2,128,20,128]{3,1,2,0:T(8,128)(2,1)}, bf16[2,128,20,128]{3,1,2,0:T(8,128)(2,1)S(1)}, u32[]{:S(2)}, u32[]{:S(2)}) collective-permute-start(bf16[2,128,20,128]{3,1,2,0:T(8,128)(2,1)} %get-tuple-element.778), channel_id=1, source_target_pairs={{0,4},{4,8},{8,12},{12,16},{16,20},{20,24},{24,28},{1,5},{5,9},{9,... | collective-permute-start | bytes 3932168 | tf_op jit(solution)/shard_map/while/body/eval_jaxpr/ppermute | solution.py:15
  38.3 1.5 collective-permute-start.1
  41.8 1.3 fusion.137
  44.0 1.8 fusion.138
  45.8 21.9 %collective-permute-done = bf16[2,128,20,128]{3,1,2,0:T(8,128)(2,1)S(1)} collective-permute-done((bf16[2,128,20,128]{3,1,2,0:T(8,128)(2,1)}, bf16[2,128,20,128]{3,1,2,0:T(8,128)(2,1)S(1)}, u32[]{:S(2)}, u32[]{:S(2)}) %collective-permute-start) | collective-permute-done | bytes 1310752 | tf_op jit(solution)/shard_map/while/body/eval_jaxpr/ppermute | solution.py:15
  69.3 3.3 fusion.143
  74.4 2.5 fusion.144
  77.4 45.4 %collective-permute-done.1 = f32[2,128,20,128]{3,1,2,0:T(8,128)} collective-permute-done((f32[2,128,20,128]{3,1,2,0:T(8,128)}, f32[2,128,20,128]{3,1,2,0:T(8,128)}, u32[]{:S(2)}, u32[]{:S(2)}) %collective-permute-start.1) | collective-permute-done | bytes 2621472 | tf_op jit(solution)/shard_map/while/body/eval_jaxpr/ppermute | solution.py:20
  122.8 3.7 maximum_add_fusion.2
  126.5 4.5 %collective-permute-start = (bf16[2,128,20,128]{3,1,2,0:T(8,128)(2,1)}, bf16[2,128,20,128]{3,1,2,0:T(8,128)(2,1)S(1)}, u32[]{:S(2)}, u32[]{:S(2)}) collective-permute-start(bf16[2,128,20,128]{3,1,2,0:T(8,128)(2,1)} %get-tuple-element.778), channel_id=1, source_target_pairs={{0,4},{4,8},{8,12},{12,16},{16,20},{20,24},{24,28},{1,5},{5,9},{9,... | collective-permute-start | bytes 3932168 | tf_op jit(solution)/shard_map/while/body/eval_jaxpr/ppermute | solution.py:15
  130.9 2.4 collective-permute-start.1
  135.3 1.3 fusion.137
  137.5 1.8 fusion.138
  139.3 21.1 %collective-permute-done = bf16[2,128,20,128]{3,1,2,0:T(8,128)(2,1)S(1)} collective-permute-done((bf16[2,128,20,128]{3,1,2,0:T(8,128)(2,1)}, bf16[2,128,20,128]{3,1,2,0:T(8,128)(2,1)S(1)}, u32[]{:S(2)}, u32[]{:S(2)}) %collective-permute-start) | collective-permute-done | bytes 1310752 | tf_op jit(solution)/shard_map/while/body/eval_jaxpr/ppermute | solution.py:15
  161.9 3.3 fusion.143
  167.1 2.5 fusion.144
  170.1 44.4 %collective-permute-done.1 = f32[2,128,20,128]{3,1,2,0:T(8,128)} collective-permute-done((f32[2,128,20,128]{3,1,2,0:T(8,128)}, f32[2,128,20,128]{3,1,2,0:T(8,128)}, u32[]{:S(2)}, u32[]{:S(2)}) %collective-permute-start.1) | collective-permute-done | bytes 2621472 | tf_op jit(solution)/shard_map/while/body/eval_jaxpr/ppermute | solution.py:20
  214.5 3.7 maximum_add_fusion.2
  218.2 4.5 %collective-permute-start = (bf16[2,128,20,128]{3,1,2,0:T(8,128)(2,1)}, bf16[2,128,20,128]{3,1,2,0:T(8,128)(2,1)S(1)}, u32[]{:S(2)}, u32[]{:S(2)}) collective-permute-start(bf16[2,128,20,128]{3,1,2,0:T(8,128)(2,1)} %get-tuple-element.778), channel_id=1, source_target_pairs={{0,4},{4,8},{8,12},{12,16},{16,20},{20,24},{24,28},{1,5},{5,9},{9,... | collective-permute-start | bytes 3932168 | tf_op jit(solution)/shard_map/while/body/eval_jaxpr/ppermute | solution.py:15
  222.7 3.3 collective-permute-start.1
  227.9 1.3 fusion.137
  230.1 1.8 fusion.138
  231.9 20.2 %collective-permute-done = bf16[2,128,20,128]{3,1,2,0:T(8,128)(2,1)S(1)} collective-permute-done((bf16[2,128,20,128]{3,1,2,0:T(8,128)(2,1)}, bf16[2,128,20,128]{3,1,2,0:T(8,128)(2,1)S(1)}, u32[]{:S(2)}, u32[]{:S(2)}) %collective-permute-start) | collective-permute-done | bytes 1310752 | tf_op jit(solution)/shard_map/while/body/eval_jaxpr/ppermute | solution.py:15
  253.6 3.3 fusion.143
  258.8 2.5 fusion.144
  261.8 43.5 %collective-permute-done.1 = f32[2,128,20,128]{3,1,2,0:T(8,128)} collective-permute-done((f32[2,128,20,128]{3,1,2,0:T(8,128)}, f32[2,128,20,128]{3,1,2,0:T(8,128)}, u32[]{:S(2)}, u32[]{:S(2)}) %collective-permute-start.1) | collective-permute-done | bytes 2621472 | tf_op jit(solution)/shard_map/while/body/eval_jaxpr/ppermute | solution.py:20
  305.3 3.7 maximum_add_fusion.2
  309.0 2.9 copy.64
  311.9 5.3 %collective-permute-start.2 = (bf16[2,128,20,128]{1,3,2,0:T(8,128)(2,1)}, bf16[2,128,20,128]{1,3,2,0:T(8,128)(2,1)S(1)}, u32[]{:S(2)}, u32[]{:S(2)}) collective-permute-start(bf16[2,128,20,128]{1,3,2,0:T(8,128)(2,1)} %copy.64), channel_id=1, source_target_pairs={{0,20},{4,24},{8,28},{12,0},{16,4},{20,8},{24,12},{28,16},{1,21},{... | collective-permute-start | bytes 3932168 | tf_op jit(solution)/shard_map/ppermute | solution.py:20
  317.3 81.3 %all-reduce = (f32[32]{0:T(128)S(1)}, f32[32]{0:T(128)S(1)}, f32[32,20]{0,1:T(8,128)S(1)}) all-reduce(f32[32]{0:T(128)S(1)} %get-tuple-element.465, f32[32]{0:T(128)S(1)} %get-tuple-element.466, f32[32,20]{0,1:T(8,128)S(1)} %get-tuple-element.467), channel_id=1, replica_groups=mesh['cp'=8,'dp'=4] {'cp','dp'}, use_global_device_ids=true, to_apply=%region_11.12 | all-reduce | flops 704 | bytes 5632 | tf_op jit(solution)/shard_map/psum | solution.py:167
  398.9 1.1 copy.65
  401.2 1.1 copy.67
  402.3 1.1 copy.66
  (94 shorter events, 21.3 us)
Async XLA Ops:
  0.6 6.6 %copy-start.5 = (bf16[1,128,2560]{2,1,0:T(8,128)(2,1)S(1)}, bf16[1,128,2560]{2,1,0:T(8,128)(2,1)}, u32[]{:S(2)}) copy-start(bf16[1,128,2560]{2,1,0:T(8,128)(2,1)} %param.14) | copy-start | bytes 1966084
  5.7 2.6 copy-start.6
  8.3 1.1 copy-start.7
  8.6 1.8 copy-start.8
  10.8 1.7 copy-start.9
  10.8 1.7 copy-start.10
  10.8 1.7 copy-start.11
  15.1 1.7 copy-start.3
  27.8 2.5 copy-start.4
  30.3 3.1 copy-start.12
  33.4 34.3 %collective-permute-start = (bf16[2,128,20,128]{3,1,2,0:T(8,128)(2,1)}, bf16[2,128,20,128]{3,1,2,0:T(8,128)(2,1)S(1)}, u32[]{:S(2)}, u32[]{:S(2)}) collective-permute-start(bf16[2,128,20,128]{3,1,2,0:T(8,128)(2,1)} %get-tuple-element.778), channel_id=1, source_target_pairs={{0,4},{4,8},{8,12},{12,16},{16,20},{20,24},{24,28},{1,5},{5,9},{9,... | collective-permute-start | bytes 3932168 | tf_op jit(solution)/shard_map/while/body/eval_jaxpr/ppermute | solution.py:15
  38.3 84.4 %collective-permute-start.1 = (f32[2,128,20,128]{3,1,2,0:T(8,128)}, f32[2,128,20,128]{3,1,2,0:T(8,128)}, u32[]{:S(2)}, u32[]{:S(2)}) collective-permute-start(f32[2,128,20,128]{3,1,2,0:T(8,128)} %get-tuple-element.779), channel_id=1, source_target_pairs={{0,4},{4,8},{8,12},{12,16},{16,20},{20,24},{24,28},{28,0},{1,5},{5... | collective-permute-start | bytes 7864328 | tf_op jit(solution)/shard_map/while/body/eval_jaxpr/ppermute | solution.py:20
  74.4 2.5 copy-start
  77.4 49.1 %copy-start.1 = (f32[128,20,128]{2,0,1:T(8,128)}, f32[128,20,128]{2,0,1:T(8,128)S(1)}, u32[]{:S(2)}) copy-start(f32[128,20,128]{2,0,1:T(8,128)S(1)} %fusion.142) | copy-start | bytes 3932164 | tf_op jit(solution)/shard_map/while
  126.5 33.9 %collective-permute-start = (bf16[2,128,20,128]{3,1,2,0:T(8,128)(2,1)}, bf16[2,128,20,128]{3,1,2,0:T(8,128)(2,1)S(1)}, u32[]{:S(2)}, u32[]{:S(2)}) collective-permute-start(bf16[2,128,20,128]{3,1,2,0:T(8,128)(2,1)} %get-tuple-element.778), channel_id=1, source_target_pairs={{0,4},{4,8},{8,12},{12,16},{16,20},{20,24},{24,28},{1,5},{5,9},{9,... | collective-permute-start | bytes 3932168 | tf_op jit(solution)/shard_map/while/body/eval_jaxpr/ppermute | solution.py:15
  130.9 83.6 %collective-permute-start.1 = (f32[2,128,20,128]{3,1,2,0:T(8,128)}, f32[2,128,20,128]{3,1,2,0:T(8,128)}, u32[]{:S(2)}, u32[]{:S(2)}) collective-permute-start(f32[2,128,20,128]{3,1,2,0:T(8,128)} %get-tuple-element.779), channel_id=1, source_target_pairs={{0,4},{4,8},{8,12},{12,16},{16,20},{20,24},{24,28},{28,0},{1,5},{5... | collective-permute-start | bytes 7864328 | tf_op jit(solution)/shard_map/while/body/eval_jaxpr/ppermute | solution.py:20
  167.1 2.5 copy-start
  170.0 48.2 %copy-start.1 = (f32[128,20,128]{2,0,1:T(8,128)}, f32[128,20,128]{2,0,1:T(8,128)S(1)}, u32[]{:S(2)}) copy-start(f32[128,20,128]{2,0,1:T(8,128)S(1)} %fusion.142) | copy-start | bytes 3932164 | tf_op jit(solution)/shard_map/while
  218.2 33.9 %collective-permute-start = (bf16[2,128,20,128]{3,1,2,0:T(8,128)(2,1)}, bf16[2,128,20,128]{3,1,2,0:T(8,128)(2,1)S(1)}, u32[]{:S(2)}, u32[]{:S(2)}) collective-permute-start(bf16[2,128,20,128]{3,1,2,0:T(8,128)(2,1)} %get-tuple-element.778), channel_id=1, source_target_pairs={{0,4},{4,8},{8,12},{12,16},{16,20},{20,24},{24,28},{1,5},{5,9},{9,... | collective-permute-start | bytes 3932168 | tf_op jit(solution)/shard_map/while/body/eval_jaxpr/ppermute | solution.py:15
  222.7 82.6 %collective-permute-start.1 = (f32[2,128,20,128]{3,1,2,0:T(8,128)}, f32[2,128,20,128]{3,1,2,0:T(8,128)}, u32[]{:S(2)}, u32[]{:S(2)}) collective-permute-start(f32[2,128,20,128]{3,1,2,0:T(8,128)} %get-tuple-element.779), channel_id=1, source_target_pairs={{0,4},{4,8},{8,12},{12,16},{16,20},{20,24},{24,28},{28,0},{1,5},{5... | collective-permute-start | bytes 7864328 | tf_op jit(solution)/shard_map/while/body/eval_jaxpr/ppermute | solution.py:20
  258.8 2.5 copy-start
  261.8 47.2 %copy-start.1 = (f32[128,20,128]{2,0,1:T(8,128)}, f32[128,20,128]{2,0,1:T(8,128)S(1)}, u32[]{:S(2)}) copy-start(f32[128,20,128]{2,0,1:T(8,128)S(1)} %fusion.142) | copy-start | bytes 3932164 | tf_op jit(solution)/shard_map/while
  309.0 89.6 %copy-start.2 = (f32[128,20,128]{2,0,1:T(8,128)S(1)}, f32[128,20,128]{2,0,1:T(8,128)}, u32[]{:S(2)}) copy-start(f32[128,20,128]{2,0,1:T(8,128)} %get-tuple-element.463) | copy-start | bytes 3932164
  311.9 89.2 %collective-permute-start.2 = (bf16[2,128,20,128]{1,3,2,0:T(8,128)(2,1)}, bf16[2,128,20,128]{1,3,2,0:T(8,128)(2,1)S(1)}, u32[]{:S(2)}, u32[]{:S(2)}) collective-permute-start(bf16[2,128,20,128]{1,3,2,0:T(8,128)(2,1)} %copy.64), channel_id=1, source_target_pairs={{0,20},{4,24},{8,28},{12,0},{16,4},{20,8},{24,12},{28,16},{1,21},{... | collective-permute-start | bytes 3932168 | tf_op jit(solution)/shard_map/ppermute | solution.py:20
where the time goes:
time: 404 us; the launch traced here: 403 us
  waiting for transfers between devices  197 us (49%)
  blocking collectives  81.3 us (20%)
  matrix products  45 us (11%)
  other arithmetic  27.9 us (7%)
  starting transfers between devices  26.4 us (7%)
  local copies, waits for them, and re-layouts  18.4 us (5%)
  loops' own time  6.22 us (2%)
    ppermute x4, waiting for transfers between devices, shifted_3(): lax.ppermute(shard, axis, [(i, (i + by) % count) for i in range(count)])  133 us
    psum x1, blocking collectives, on_device(): first, bias_sum, second = lax.psum((first, bias_sum, second), ('cp', 'dp'))  81.3 us
    ppermute x3, waiting for transfers between devices, shifted_2(): return lax.ppermute(block, axis, route)  63.2 us
    ppermute x3, starting transfers between devices, shifted_2(): return lax.ppermute(block, axis, route)  13.8 us
    dot_general x4, matrix products, pair_terms(): grad_act = jnp.einsum('hqk,ch->cqk', dscore, fire_w2, precision=highest)  13.1 us
    ppermute x4, starting transfers between devices, shifted_3(): lax.ppermute(shard, axis, [(i, (i + by) % count) for i in range(count)])  12.6 us
    unnamed x34, local copies, waits for them, and re-layouts  11.9 us
    add x3, other arithmetic, carried_hop(): moving_grads = moving_grads + jnp.stack([terms[1], terms[2]])  11.1 us
  transfers between devices with their start and end apart: 7, of which 6 were waited for; matrix products, arithmetic and copies ran while one was open for 11% of the time, Pallas kernels for 0%

commit v1 on v0

--- a/solution.py
+++ b/solution.py
@@ -1,6 +1,8 @@
 import jax
 import jax.numpy as jnp
 from jax import lax
+from jax.experimental import pallas as pl
+from jax.experimental.pallas import tpu as pltpu
 from jax.sharding import PartitionSpec as P
 
 GROUP_MOST = 4
@@ -87,6 +89,341 @@
     return shifted_2(key_value, "cp", 1)
 
 
+MESH = pl.DeviceIdType.MESH
+NT = (((1,), (1,)), ((), ()))
+NN = (((1,), (0,)), ((), ()))
+TN = (((0,), (0,)), ((), ()))
+MASKED = -1e30
+BIAS_ROWS = 32
+SUM_ROWS = 16
+
+
+def exchange_kernel(
+    q_ref,
+    k_ref,
+    v_ref,
+    g_ref,
+    stat_ref,
+    start_ref,
+    rden_ref,
+    w1_ref,
+    b1_ref,
+    w2_ref,
+    dq_ref,
+    dk_ref,
+    dv_ref,
+    sums_ref,
+    held,
+    stats,
+    pair,
+    ratios,
+    grads,
+    acc,
+    send_in,
+    recv_in,
+    send_stat,
+    recv_stat,
+    send_out,
+    recv_out,
+):
+    parts = GROUP_MOST
+    heads, tokens, size = held.shape[1:]
+    rows = tokens // parts
+    hidden = w1_ref.shape[0]
+    scale_value = size ** (-0.5)
+    me = lax.axis_index("cp")
+    rank = lax.rem(me, parts)
+    base = me - rank
+    inputs = (q_ref, k_ref, v_ref, g_ref)
+    results = (dq_ref, dk_ref, dv_ref)
+
+    def peer_of(step):
+        return lax.rem(rank + step, parts)
+
+    def row_block(index):
+        return pl.ds(pl.multiple_of(index * rows, rows), rows)
+
+    def head_columns(part, head):
+        return pl.ds(pl.multiple_of((part * heads + head) * size, size), size)
+
+    def stat_copy(step):
+        peer = peer_of(step)
+        return pltpu.make_async_remote_copy(
+            src_ref=stat_ref.at[peer],
+            dst_ref=stats.at[rank],
+            send_sem=send_stat.at[step - 1],
+            recv_sem=recv_stat.at[step - 1],
+            device_id={"cp": base + peer},
+            device_id_type=MESH,
+        )
+
+    def in_copy(array, head, step):
+        peer = peer_of(step)
+        return pltpu.make_async_remote_copy(
+            src_ref=inputs[array].at[:, head_columns(peer, head)],
+            dst_ref=held.at[array, head, row_block(rank), :],
+            send_sem=send_in.at[array, head, step - 1],
+            recv_sem=recv_in.at[array, head, step - 1],
+            device_id={"cp": base + peer},
+            device_id_type=MESH,
+        )
+
+    def out_copy(array, head, step):
+        peer = peer_of(step)
+        return pltpu.make_async_remote_copy(
+            src_ref=grads.at[array, head, row_block(peer), :],
+            dst_ref=results[array].at[:, head_columns(rank, head)],
+            send_sem=send_out.at[array, head, step - 1],
+            recv_sem=recv_out.at[array, head, step - 1],
+            device_id={"cp": base + peer},
+            device_id_type=MESH,
+        )
+
+    barrier = pltpu.get_barrier_semaphore()
+    for step in range(1, parts):
+        pl.semaphore_signal(
+            barrier, inc=1, device_id={"cp": base + peer_of(step)}, device_id_type=MESH
+        )
+    pl.semaphore_wait(barrier, parts - 1)
+
+    for step in range(1, parts):
+        stat_copy(step).start()
+
+    def send_head(head, carry):
+        for step in (2, 1, 3):
+            for array in range(4):
+                in_copy(array, head, step).start()
+        return carry
+
+    lax.fori_loop(0, heads, send_head, 0)
+
+    stats[rank] = stat_ref[rank]
+
+    def own_head(head, carry):
+        for array in range(4):
+            held[array, head, row_block(rank), :] = inputs[array][:, head_columns(rank, head)]
+        return carry
+
+    lax.fori_loop(0, heads, own_head, 0)
+
+    def bias_column(block, carry):
+        columns = row_block(block)
+        start = start_ref[:, columns]
+        rden = rden_ref[:, columns]
+
+        def bias_rows(chunk, carry):
+            at = pl.ds(pl.multiple_of(chunk * BIAS_ROWS, BIAS_ROWS), BIAS_ROWS)
+            key_at = chunk * BIAS_ROWS + lax.broadcasted_iota(jnp.int32, (BIAS_ROWS, rows), 0)
+            query_at = block * rows + lax.broadcasted_iota(jnp.int32, (BIAS_ROWS, rows), 1)
+            allowed = (key_at >= start) & (key_at <= query_at)
+            distance = jnp.maximum(query_at - key_at, 0).astype(jnp.float32)
+            ratio = jnp.log(1.0 + distance) * rden
+            ratios[at, columns] = ratio
+            totals = [jnp.zeros((BIAS_ROWS, rows), jnp.float32) for _ in range(heads)]
+            for unit in range(hidden):
+                act = jnp.maximum(ratio * w1_ref[unit] + b1_ref[unit], 0.0)
+                for head in range(heads):
+                    totals[head] = totals[head] + act * w2_ref[unit, head]
+            for head in range(heads):
+                pair[head, at, columns] = jnp.where(allowed, totals[head], MASKED)
+            return carry
+
+        return lax.fori_loop(0, (block + 1) * (rows // BIAS_ROWS), bias_rows, carry)
+
+    lax.fori_loop(0, parts, bias_column, 0)
+    half = 2 * rows
+    for head in range(heads):
+        for first in range(0, parts, 2):
+            pair[head, (first + 1) * rows : (first + 2) * rows, first * rows : (first + 1) * rows] = (
+                jnp.full((rows, rows), MASKED, jnp.float32)
+            )
+    acc[...] = jnp.zeros_like(acc)
+
+    for step in range(1, parts):
+        stat_copy(step).wait_recv()
+
+    def one_head(head, carry):
+        for step in (2, 1, 3):
+            for array in range(4):
+                in_copy(array, head, step).wait_recv()
+        log_row = jnp.concatenate(
+            [stats[part, pl.ds(head, 1), :] for part in range(parts)], axis=1
+        )
+        delta_row = jnp.concatenate(
+            [stats[part, pl.ds(8 + head, 1), :] for part in range(parts)], axis=1
+        )
+
+        def dot(a, b, dims):
+            return lax.dot_general(a, b, dims, preferred_element_type=jnp.float32)
+
+        dq = [None, None]
+        dk = [None, None]
+        dv = [None, None]
+
+        def plus(total, term):
+            return term if total is None else total + term
+
+        for kt, qt in ((0, 0), (0, 1), (1, 1)):
+            krows = slice(kt * half, (kt + 1) * half)
+            qrows = slice(qt * half, (qt + 1) * half)
+            q = held[0, head, qrows, :]
+            k = held[1, head, krows, :]
+            v = held[2, head, krows, :]
+            g = held[3, head, qrows, :]
+            scores = dot(k, q, NT) * scale_value + pair[head, krows, qrows]
+            prob = jnp.exp(scores - log_row[:, qrows])
+            dscore = prob * (dot(v, g, NT) - delta_row[:, qrows])
+            pair[head, krows, qrows] = dscore
+            prob_low = prob.astype(jnp.bfloat16)
+            score_low = dscore.astype(jnp.bfloat16)
+            dv[kt] = plus(dv[kt], dot(prob_low, g, NN))
+            dk[kt] = plus(dk[kt], dot(score_low, q, NN))
+            dq[qt] = plus(dq[qt], dot(score_low, k, TN))
+        for tile in range(2):
+            trows = slice(tile * half, (tile + 1) * half)
+            grads[0, head, trows, :] = (dq[tile] * scale_value).astype(jnp.bfloat16)
+            grads[1, head, trows, :] = (dk[tile] * scale_value).astype(jnp.bfloat16)
+            grads[2, head, trows, :] = dv[tile].astype(jnp.bfloat16)
+        for step in (2, 1, 3):
+            for array in range(3):
+                out_copy(array, head, step).start()
+        for array in range(3):
+            results[array][:, head_columns(rank, head)] = grads[array, head, row_block(rank), :]
+        return carry
+
+    lax.fori_loop(0, heads, one_head, 0)
+
+    def sum_column(block, carry):
+        columns = row_block(block)
+
+        def sum_rows(chunk, carry):
+            at = pl.ds(pl.multiple_of(chunk * SUM_ROWS, SUM_ROWS), SUM_ROWS)
+            ratio = ratios[at, columns]
+            flat = [pair[head, at, columns] for head in range(heads)]
+            tilted = [term * ratio for term in flat]
+            for unit in range(hidden):
+                live = ratio * w1_ref[unit] > -b1_ref[unit]
+                for head in range(heads):
+                    for kind, term in ((0, flat[head]), (1, tilted[head])):
+                        kept = jnp.where(live, term, 0.0)
+                        part = kept[0:8]
+                        for row in range(8, SUM_ROWS, 8):
+                            part = part + kept[row : row + 8]
+                        acc[kind, head, unit] += part
+            return carry
+
+        return lax.fori_loop(0, (block + 1) * (rows // SUM_ROWS), sum_rows, carry)
+
+    lax.fori_loop(0, parts, sum_column, 0)
+    for kind in range(2):
+        for head in range(heads):
+            sums_ref[kind, head] = jnp.sum(acc[kind, head], axis=1)
+
+    def drain_head(head, carry):
+        for step in (2, 1, 3):
+            for array in range(4):
+                in_copy(array, head, step).wait_send()
+            for array in range(3):
+                out_copy(array, head, step).wait()
+        return carry
+
+    lax.fori_loop(0, heads, drain_head, 0)
+    for step in range(1, parts):
+        stat_copy(step).wait_send()
+
+
+def by_heads(queries, keys, values, outputs, d_out, log_norm, lengths, fire_w1, fire_b1, fire_w2):
+    rows_dev = queries.shape[1]
+    heads_count = log_norm.shape[2]
+    feature_count = queries.shape[2]
+    head_size = feature_count // heads_count
+    cp_count = lax.axis_size("cp")
+    parts = GROUP_MOST
+    heads = heads_count // parts
+    hidden = fire_w1.shape[0]
+    tokens = parts * rows_dev
+    me = lax.axis_index("cp")
+    rank = lax.rem(me, parts)
+    base = me - rank
+    delta = jnp.einsum(
+        "qhd,qhd->hq",
+        d_out[0].reshape(rows_dev, heads_count, head_size),
+        outputs[0].reshape(rows_dev, heads_count, head_size),
+        preferred_element_type=jnp.float32,
+    )
+    pad = ((0, 0), (0, 8 - heads), (0, 0))
+    stat = jnp.concatenate(
+        [
+            jnp.pad(log_norm[0].T.reshape(parts, heads, rows_dev), pad),
+            jnp.pad(delta.reshape(parts, heads, rows_dev), pad),
+        ],
+        axis=1,
+    )
+    ends = jnp.cumsum(lengths[0])
+    begins = ends - lengths[0]
+    blocks = base + jnp.arange(parts, dtype=jnp.int32)
+    mine = (begins[None, :] <= blocks[:, None]) & (blocks[:, None] < ends[None, :])
+    begin = (jnp.sum(jnp.where(mine, begins[None, :], 0), axis=1) - base) * rows_dev
+    start = jnp.repeat(begin, rows_dev)[None, :]
+    position = (jnp.arange(tokens, dtype=jnp.int32)[None, :] - start).astype(jnp.float32)
+    rden = 1.0 / jnp.log1p(jnp.maximum(position, fire_floor))
+    w2_mine = lax.dynamic_slice(fire_w2, (0, rank * heads), (hidden, heads))
+
+    vmem = pl.BlockSpec(memory_space=pltpu.VMEM)
+    smem = pl.BlockSpec(memory_space=pltpu.SMEM)
+    low = jnp.bfloat16
+    block = jax.ShapeDtypeStruct((rows_dev, feature_count), low)
+    steps = parts - 1
+    dma = pltpu.SemaphoreType.DMA
+    grad_q, grad_k, grad_v, sums = pl.pallas_call(
+        exchange_kernel,
+        out_shape=(
+            block,
+            block,
+            block,
+            jax.ShapeDtypeStruct((2, heads, hidden, 128), jnp.float32),
+        ),
+        in_specs=[vmem] * 7 + [smem] * 3,
+        out_specs=(vmem,) * 4,
+        scratch_shapes=[
+            pltpu.VMEM((4, heads, tokens, head_size), low),
+            pltpu.VMEM((parts, 16, rows_dev), jnp.float32),
+            pltpu.VMEM((heads, tokens, tokens), jnp.float32),
+            pltpu.VMEM((tokens, tokens), jnp.float32),
+            pltpu.VMEM((3, heads, tokens, head_size), low),
+            pltpu.VMEM((2, heads, hidden, 8, 128), jnp.float32),
+            dma((4, heads, steps)),
+            dma((4, heads, steps)),
+            dma((steps,)),
+            dma((steps,)),
+            dma((3, heads, steps)),
+            dma((3, heads, steps)),
+        ],
+        compiler_params=pltpu.CompilerParams(
+            collective_id=0, has_side_effects=True, vmem_limit_bytes=48 * 2**20
+        ),
+    )(queries[0], keys[0], values[0], d_out[0], stat, start, rden, fire_w1, fire_b1, w2_mine)
+    sums = jnp.sum(sums, axis=3)
+    flat, tilted = sums[0].T, sums[1].T
+    second = jnp.zeros((hidden, heads_count), jnp.float32)
+    second = lax.dynamic_update_slice(
+        second, fire_w1[:, None] * tilted + fire_b1[:, None] * flat, (0, rank * heads)
+    )
+    first = jnp.sum(w2_mine * tilted, axis=1)
+    bias_sum = jnp.sum(w2_mine * flat, axis=1)
+    joined = jnp.concatenate([second, first[:, None], bias_sum[:, None]], axis=1)
+    factor = (lax.axis_size("dp") * cp_count * rows_dev) ** (-0.5)
+    joined = lax.psum(joined, ("cp", "dp")) * factor
+    return (
+        grad_q[None],
+        grad_k[None],
+        grad_v[None],
+        joined[:, heads_count],
+        joined[:, heads_count + 1],
+        joined[:, :heads_count],
+    )
+
+
 def on_device(queries, keys, values, outputs, d_out, log_norm, lengths, fire_w1, fire_b1, fire_w2):
     rows_dev = queries.shape[1]
     heads_count = log_norm.shape[2]
@@ -190,8 +527,9 @@
         P(),
         P(),
     )
+    plan = by_heads if mesh.shape["cp"] == 2 * GROUP_MOST else on_device
     return jax.shard_map(
-        on_device,
+        plan,
         mesh=mesh,
         in_specs=placed,
         out_specs=(P("dp", "cp", None), P("dp", "cp", None), P("dp", "cp", None), P(), P(), P()),

time: 404 us -> 110 us (0.27)
  waiting for transfers between devices: 197 us -> 0 us
  Pallas kernels: 0 us -> 57.2 us
  matrix products: 45 us -> 0 us
  blocking collectives: 81.3 us -> 40.7 us
  starting transfers between devices: 26.4 us -> 0 us
  other arithmetic: 27.9 us -> 2.18 us
  local copies, waits for them, and re-layouts: 18.4 us -> 9.06 us
  loops' own time: 6.22 us -> 0 us
    ppermute x7 -> x0, waiting for transfers between devices: 197 us -> none  [the longest x4 133 us: shifted_3(): lax.ppermute(shard, axis, [(i, (i + by) % count) for i in range(count)])]
    pallas_call x0 -> x1, Pallas kernels: none -> 57.2 us  [by_heads(): pl.pallas_call(exchange_kernel, out_shape=(block, block, block, jax.Shape...]
    dot_general x32 -> x0, matrix products: 45 us -> none  [the longest x4 13.1 us: pair_terms(): grad_act = jnp.einsum('hqk,ch->cqk', dscore, fire_w2, precision=highest)]
    psum x1, blocking collectives: 81.3 us -> 40.7 us  [by_heads(): joined = lax.psum(joined, ('cp', 'dp')) * factor]
    ppermute x7 -> x0, starting transfers between devices: 26.4 us -> none  [the longest x3 13.8 us: shifted_2(): return lax.ppermute(block, axis, route)]
    add x16 -> x1, other arithmetic: 11.2 us -> 0.01 us  [by_heads(): blocks = base + jnp.arange(parts, dtype=jnp.int32)]
    reduce_sum x8 -> x3, other arithmetic: 8.29 us -> 0.43 us  [the longest x1 0.18 us: by_heads(): jnp.sum(jnp.where(mine, begins[None, :], 0), axis=1) - base]
    while x17 -> x0, local copies, waits for them, and re-layouts: 6.44 us -> none  [the longest x2 3.23 us: on_device(): result = lax.fori_loop(1, GROUP_MOST, carried_hop, start)]
  transfers between devices with their start and end apart: 7 -> 0, of which waited for: 6 -> 0; matrix products, arithmetic and copies ran while one was open for 11% -> 0% of each run, Pallas kernels for 0% -> 0%
where the time goes in v1:
time: 110 us
  Pallas kernels  57.2 us (52%)
  blocking collectives  40.7 us (37%)
  local copies, waits for them, and re-layouts  9.06 us (8%)
  other arithmetic  2.18 us (2%)
    pallas_call x1, Pallas kernels, by_heads(): pl.pallas_call(exchange_kernel, out_shape=(block, block, block, jax.Shape...  57.2 us
    psum x1, blocking collectives, by_heads(): joined = lax.psum(joined, ('cp', 'dp')) * factor  40.7 us
    unnamed x27, local copies, waits for them, and re-layouts  8.29 us

profile of v1, /device:TPU:0, one launch (start us, length us, event | category | flops | bytes accessed | tf_op | source)
XLA Modules:
  0.0 109.9 jit_solution(4356804073701231928)
XLA Ops:
  0.6 0.0 copy-start
  0.7 0.7 copy-done
  1.4 0.1 copy.52.w2_ref
  1.4 0.8 reduce-window.4
  2.3 0.7 fusion.4
  2.9 0.2 select_reduce_fusion
  3.1 0.1 broadcast_in_dim.40
  3.2 0.0 copy-start.1
  3.2 1.5 %copy.49 = bf16[1,128,2560]{1,2,0:T(8,128)(2,1)S(1)} copy(bf16[1,128,2560]{2,1,0:T(8,128)(2,1)} %param.13) | data formatting | bytes 1310720
  4.7 0.0 copy-done.1
  4.7 0.3 copy.50
  5.1 0.0 copy-start.8
  5.1 0.0 copy-start.2
  5.1 0.0 copy-start.5
  5.1 0.0 copy-start.6
  5.1 0.2 fusion
  5.3 0.4 copy-done.8
  5.8 0.4 copy-done.2
  6.2 0.0 copy-done.5
  6.2 0.0 copy-done.6
  6.2 0.0 copy-start.3
  6.2 1.1 copy-done.3
  7.3 0.0 copy-start.4
  7.3 1.1 copy-done.4
  8.3 57.2 %shard_map.145 = (bf16[128,2560]{1,0:T(8,128)(2,1)S(1)}, bf16[128,2560]{1,0:T(8,128)(2,1)S(1)}, bf16[128,2560]{1,0:T(8,128)(2,1)S(1)}, f32[2,5,32,128]{3,2,1,0:T(8,128)S(1)}) custom-call(bf16[128,2560]{1,0:T(8,128)(2,1)S(1)} %bitcast.59, bf16[128,2560]{1,0:T(8,128)(2,1)S(1)} %bitcast.60, bf16[128,2560]{1,0:T(8,128)(2,1)S(1)} %bitcast.61, ...), custom_call_target="tpu_custom_call" | custom-call | tf_op jit(solution)/shard_map/pallas_call | solution.py:378
  65.5 0.1 reduce_sum.37
  65.7 0.1 copy.53
  65.8 0.1 copy.54
  65.8 0.1 fusion.3
  66.0 0.1 copy.40
  66.1 0.1 dynamic_update_slice.3
  66.2 40.7 %psum.7 = f32[32,22]{0,1:T(8,128)S(1)} all-reduce(f32[32,22]{0,1:T(8,128)S(1)} %pad_maximum_fusion), channel_id=1, replica_groups=mesh['cp'=8,'dp'=4] {'cp','dp'}, use_global_device_ids=true, to_apply=%region_5.6 | all-reduce | flops 704 | bytes 5632 | tf_op jit(solution)/shard_map/psum | solution.py:416
  106.9 0.0 copy-start.7
  106.9 0.5 slice_bitcast_fusion
  107.4 0.8 copy.62
  108.2 0.0 copy-done.7
  108.2 0.8 copy.63
  109.1 0.8 copy.64
  (12 shorter events, 0.1 us)
Async XLA Ops:
  0.6 0.7 copy-start
  3.2 1.5 %copy-start.1 = (bf16[1,128,2560]{2,1,0:T(8,128)(2,1)S(1)}, bf16[1,128,2560]{2,1,0:T(8,128)(2,1)}, u32[]{:S(2)}) copy-start(bf16[1,128,2560]{2,1,0:T(8,128)(2,1)} %param.14) | copy-start | bytes 1966084
  5.1 0.7 copy-start.8
  5.1 1.1 copy-start.2
  5.1 1.1 copy-start.5
  5.1 1.1 copy-start.6
  6.2 1.1 copy-start.3
  7.3 1.1 copy-start.4
  106.9 1.4 %copy-start.7 = (f32[32,22]{0,1:T(8,128)}, f32[32,22]{0,1:T(8,128)S(1)}, u32[]{:S(2)}) copy-start(f32[32,22]{0,1:T(8,128)S(1)} %broadcast_multiply_fusion) | copy-start | bytes 8452

commit v2 on v1

--- a/solution.py
+++ b/solution.py
@@ -95,7 +95,7 @@
 TN = (((0,), (0,)), ((), ()))
 MASKED = -1e30
 BIAS_ROWS = 32
-SUM_ROWS = 16
+SUM_ROWS = 32
 
 
 def exchange_kernel(
@@ -103,9 +103,9 @@
     k_ref,
     v_ref,
     g_ref,
-    stat_ref,
-    start_ref,
-    rden_ref,
+    o_ref,
+    log_ref,
+    lengths_ref,
     w1_ref,
     b1_ref,
     w2_ref,
@@ -114,29 +114,48 @@
     dv_ref,
     sums_ref,
     held,
+    own_g,
+    own_o,
+    padded,
     stats,
     pair,
     ratios,
     grads,
     acc,
+    lanes,
+    cp_slots,
+    dp_slots,
+    own_sem,
+    delta_sem,
     send_in,
     recv_in,
     send_stat,
     recv_stat,
     send_out,
     recv_out,
+    send_cp,
+    recv_cp,
+    send_dp,
+    recv_dp,
 ):
     parts = GROUP_MOST
     heads, tokens, size = held.shape[1:]
     rows = tokens // parts
     hidden = w1_ref.shape[0]
+    heads_count = heads * parts
+    delta_at = stats.shape[1] // 2
+    cp_count, dp_count = cp_slots.shape[0], dp_slots.shape[0]
     scale_value = size ** (-0.5)
     me = lax.axis_index("cp")
+    my_dp = lax.axis_index("dp")
     rank = lax.rem(me, parts)
     base = me - rank
     inputs = (q_ref, k_ref, v_ref, g_ref)
     results = (dq_ref, dk_ref, dv_ref)
 
+    def dot(a, b, dims):
+        return lax.dot_general(a, b, dims, preferred_element_type=jnp.float32)
+
     def peer_of(step):
         return lax.rem(rank + step, parts)
 
@@ -147,13 +166,12 @@
         return pl.ds(pl.multiple_of((part * heads + head) * size, size), size)
 
     def stat_copy(step):
-        peer = peer_of(step)
         return pltpu.make_async_remote_copy(
-            src_ref=stat_ref.at[peer],
+            src_ref=stats.at[rank],
             dst_ref=stats.at[rank],
             send_sem=send_stat.at[step - 1],
             recv_sem=recv_stat.at[step - 1],
-            device_id={"cp": base + peer},
+            device_id={"cp": base + peer_of(step)},
             device_id_type=MESH,
         )
 
@@ -168,6 +186,13 @@
             device_id_type=MESH,
         )
 
+    def own_copy(array, head):
+        return pltpu.make_async_copy(
+            inputs[array].at[:, head_columns(rank, head)],
+            held.at[array, head, row_block(rank), :],
+            own_sem.at[array, head],
+        )
+
     def out_copy(array, head, step):
         peer = peer_of(step)
         return pltpu.make_async_remote_copy(
@@ -179,37 +204,88 @@
             device_id_type=MESH,
         )
 
+    def cp_copy(step):
+        return pltpu.make_async_remote_copy(
+            src_ref=cp_slots.at[me],
+            dst_ref=cp_slots.at[me],
+            send_sem=send_cp.at[step - 1],
+            recv_sem=recv_cp.at[step - 1],
+            device_id={"cp": lax.rem(me + step, cp_count)},
+            device_id_type=MESH,
+        )
+
+    def dp_copy(step):
+        return pltpu.make_async_remote_copy(
+            src_ref=dp_slots.at[my_dp],
+            dst_ref=dp_slots.at[my_dp],
+            send_sem=send_dp.at[step - 1],
+            recv_sem=recv_dp.at[step - 1],
+            device_id={"dp": lax.rem(my_dp + step, dp_count)},
+            device_id_type=MESH,
+        )
+
+    delta_copies = (
+        pltpu.make_async_copy(g_ref, own_g, delta_sem.at[0]),
+        pltpu.make_async_copy(o_ref, own_o, delta_sem.at[1]),
+    )
+    for copy in delta_copies:
+        copy.start()
+
     barrier = pltpu.get_barrier_semaphore()
-    for step in range(1, parts):
+    for step in range(1, cp_count):
         pl.semaphore_signal(
-            barrier, inc=1, device_id={"cp": base + peer_of(step)}, device_id_type=MESH
-        )
-    pl.semaphore_wait(barrier, parts - 1)
-
-    for step in range(1, parts):
-        stat_copy(step).start()
+            barrier, inc=1, device_id={"cp": lax.rem(me + step, cp_count)}, device_id_type=MESH
+        )
+    for step in range(1, dp_count):
+        pl.semaphore_signal(
+            barrier, inc=1, device_id={"dp": lax.rem(my_dp + step, dp_count)}, device_id_type=MESH
+        )
+    pl.semaphore_wait(barrier, cp_count + dp_count - 2)
 
     def send_head(head, carry):
         for step in (2, 1, 3):
             for array in range(4):
                 in_copy(array, head, step).start()
+        for array in range(4):
+            own_copy(array, head).start()
         return carry
 
-    lax.fori_loop(0, heads, send_head, 0)
-
-    stats[rank] = stat_ref[rank]
-
-    def own_head(head, carry):
-        for array in range(4):
-            held[array, head, row_block(rank), :] = inputs[array][:, head_columns(rank, head)]
+    early = 2
+    lax.fori_loop(0, early, send_head, 0)
+
+    padded[...] = jnp.zeros_like(padded)
+    padded[:, 0:heads_count] = log_ref[...]
+    stats[rank] = jnp.zeros(stats.shape[1:], jnp.float32)
+    stats[rank, 0:delta_at, :] = padded[...].T[0:delta_at]
+    for copy in delta_copies:
+        copy.wait()
+    ones = jnp.ones((8, 2 * size), jnp.bfloat16)
+
+    def delta_head(head, carry):
+        columns = pl.ds(pl.multiple_of(head * size, size), size)
+        product = own_g[:, columns].astype(jnp.float32) * own_o[:, columns].astype(jnp.float32)
+        high = product.astype(jnp.bfloat16)
+        rest = (product - high.astype(jnp.float32)).astype(jnp.bfloat16)
+        row = dot(ones, jnp.concatenate([high, rest], axis=1), NT)
+        stats[rank, pl.ds(delta_at + head, 1), :] = row[0:1]
         return carry
 
-    lax.fori_loop(0, heads, own_head, 0)
+    lax.fori_loop(0, heads_count, delta_head, 0)
+    for step in range(1, parts):
+        stat_copy(step).start()
+    lax.fori_loop(early, heads, send_head, 0)
 
     def bias_column(block, carry):
         columns = row_block(block)
-        start = start_ref[:, columns]
-        rden = rden_ref[:, columns]
+        start = jnp.int32(0)
+        end = jnp.int32(0)
+        for index in range(lengths_ref.shape[1]):
+            start = jnp.where(end <= base + block, end, start)
+            end = end + lengths_ref[0, index]
+        start = (start - base) * rows
+        query_row = block * rows + lax.broadcasted_iota(jnp.int32, (1, rows), 1)
+        position = (query_row - start).astype(jnp.float32)
+        rden = 1.0 / jnp.log(1.0 + jnp.maximum(position, fire_floor))
 
         def bias_rows(chunk, carry):
             at = pl.ds(pl.multiple_of(chunk * BIAS_ROWS, BIAS_ROWS), BIAS_ROWS)
@@ -223,7 +299,7 @@
             for unit in range(hidden):
                 act = jnp.maximum(ratio * w1_ref[unit] + b1_ref[unit], 0.0)
                 for head in range(heads):
-                    totals[head] = totals[head] + act * w2_ref[unit, head]
+                    totals[head] = totals[head] + act * w2_ref[unit, rank * heads + head]
             for head in range(heads):
                 pair[head, at, columns] = jnp.where(allowed, totals[head], MASKED)
             return carry
@@ -243,18 +319,16 @@
         stat_copy(step).wait_recv()
 
     def one_head(head, carry):
+        for array in range(4):
+            own_copy(array, head).wait()
         for step in (2, 1, 3):
             for array in range(4):
                 in_copy(array, head, step).wait_recv()
-        log_row = jnp.concatenate(
-            [stats[part, pl.ds(head, 1), :] for part in range(parts)], axis=1
-        )
+        at = rank * heads + head
+        log_row = jnp.concatenate([stats[part, pl.ds(at, 1), :] for part in range(parts)], axis=1)
         delta_row = jnp.concatenate(
-            [stats[part, pl.ds(8 + head, 1), :] for part in range(parts)], axis=1
-        )
-
-        def dot(a, b, dims):
-            return lax.dot_general(a, b, dims, preferred_element_type=jnp.float32)
+            [stats[part, pl.ds(delta_at + at, 1), :] for part in range(parts)], axis=1
+        )
 
         dq = [None, None]
         dk = [None, None]
@@ -291,33 +365,70 @@
             results[array][:, head_columns(rank, head)] = grads[array, head, row_block(rank), :]
         return carry
 
-    lax.fori_loop(0, heads, one_head, 0)
-
-    def sum_column(block, carry):
-        columns = row_block(block)
-
-        def sum_rows(chunk, carry):
-            at = pl.ds(pl.multiple_of(chunk * SUM_ROWS, SUM_ROWS), SUM_ROWS)
-            ratio = ratios[at, columns]
-            flat = [pair[head, at, columns] for head in range(heads)]
-            tilted = [term * ratio for term in flat]
-            for unit in range(hidden):
-                live = ratio * w1_ref[unit] > -b1_ref[unit]
-                for head in range(heads):
-                    for kind, term in ((0, flat[head]), (1, tilted[head])):
-                        kept = jnp.where(live, term, 0.0)
-                        part = kept[0:8]
-                        for row in range(8, SUM_ROWS, 8):
-                            part = part + kept[row : row + 8]
-                        acc[kind, head, unit] += part
-            return carry
-
-        return lax.fori_loop(0, (block + 1) * (rows // SUM_ROWS), sum_rows, carry)
-
-    lax.fori_loop(0, parts, sum_column, 0)
-    for kind in range(2):
+    def sum_heads(some):
+        def sum_column(block, carry):
+            columns = row_block(block)
+
+            def sum_rows(chunk, carry):
+                at = pl.ds(pl.multiple_of(chunk * SUM_ROWS, SUM_ROWS), SUM_ROWS)
+                ratio = ratios[at, columns]
+                flat = {head: pair[head, at, columns] for head in some}
+                tilted = {head: flat[head] * ratio for head in some}
+                for unit in range(hidden):
+                    live = ratio * w1_ref[unit] > -b1_ref[unit]
+                    for head in some:
+                        for kind, term in ((0, flat[head]), (1, tilted[head])):
+                            kept = jnp.where(live, term, 0.0)
+                            part = kept[0:8]
+                            for row in range(8, SUM_ROWS, 8):
+                                part = part + kept[row : row + 8]
+                            acc[kind, head, unit] += part
+                return carry
+
+            return lax.fori_loop(0, (block + 1) * (rows // SUM_ROWS), sum_rows, carry)
+
+        lax.fori_loop(0, parts, sum_column, 0)
+
+    lax.fori_loop(0, early, one_head, 0)
+    sum_heads(range(0, early))
+    lax.fori_loop(early, heads, one_head, 0)
+    sum_heads(range(early, heads))
+
+    for unit in range(hidden):
+        first = jnp.zeros((8, 128), jnp.float32)
+        bias_sum = jnp.zeros((8, 128), jnp.float32)
         for head in range(heads):
-            sums_ref[kind, head] = jnp.sum(acc[kind, head], axis=1)
+            flat, tilted = acc[0, head, unit], acc[1, head, unit]
+            weight = w2_ref[unit, rank * heads + head]
+            first = first + tilted * weight
+            bias_sum = bias_sum + flat * weight
+            second = tilted * w1_ref[unit] + flat * b1_ref[unit]
+            lanes[head, unit : unit + 1, :] = jnp.sum(second, axis=0, keepdims=True)
+        lanes[heads, unit : unit + 1, :] = jnp.sum(first, axis=0, keepdims=True)
+        lanes[heads + 1, unit : unit + 1, :] = jnp.sum(bias_sum, axis=0, keepdims=True)
+    lane = lax.broadcasted_iota(jnp.int32, (hidden, 128), 1)
+    message = jnp.zeros((hidden, 128), jnp.float32)
+    for index in range(heads + 2):
+        place = rank * heads + index if index < heads else heads_count + index - heads
+        column = jnp.sum(lanes[index], axis=1, keepdims=True)
+        message = jnp.where(lane == place, column, message)
+    cp_slots[me] = message
+    for step in range(1, cp_count):
+        cp_copy(step).start()
+    for step in range(1, cp_count):
+        cp_copy(step).wait()
+    total = cp_slots[0]
+    for index in range(1, cp_count):
+        total = total + cp_slots[index]
+    dp_slots[my_dp] = total
+    for step in range(1, dp_count):
+        dp_copy(step).start()
+    for step in range(1, dp_count):
+        dp_copy(step).wait()
+    total = dp_slots[0]
+    for index in range(1, dp_count):
+        total = total + dp_slots[index]
+    sums_ref[...] = total * (dp_count * cp_count * rows) ** (-0.5)
 
     def drain_head(head, carry):
         for step in (2, 1, 3):
@@ -337,90 +448,74 @@
     heads_count = log_norm.shape[2]
     feature_count = queries.shape[2]
     head_size = feature_count // heads_count
-    cp_count = lax.axis_size("cp")
+    cp_count, dp_count = lax.axis_size("cp"), lax.axis_size("dp")
     parts = GROUP_MOST
     heads = heads_count // parts
     hidden = fire_w1.shape[0]
     tokens = parts * rows_dev
-    me = lax.axis_index("cp")
-    rank = lax.rem(me, parts)
-    base = me - rank
-    delta = jnp.einsum(
-        "qhd,qhd->hq",
-        d_out[0].reshape(rows_dev, heads_count, head_size),
-        outputs[0].reshape(rows_dev, heads_count, head_size),
-        preferred_element_type=jnp.float32,
-    )
-    pad = ((0, 0), (0, 8 - heads), (0, 0))
-    stat = jnp.concatenate(
-        [
-            jnp.pad(log_norm[0].T.reshape(parts, heads, rows_dev), pad),
-            jnp.pad(delta.reshape(parts, heads, rows_dev), pad),
-        ],
-        axis=1,
-    )
-    ends = jnp.cumsum(lengths[0])
-    begins = ends - lengths[0]
-    blocks = base + jnp.arange(parts, dtype=jnp.int32)
-    mine = (begins[None, :] <= blocks[:, None]) & (blocks[:, None] < ends[None, :])
-    begin = (jnp.sum(jnp.where(mine, begins[None, :], 0), axis=1) - base) * rows_dev
-    start = jnp.repeat(begin, rows_dev)[None, :]
-    position = (jnp.arange(tokens, dtype=jnp.int32)[None, :] - start).astype(jnp.float32)
-    rden = 1.0 / jnp.log1p(jnp.maximum(position, fire_floor))
-    w2_mine = lax.dynamic_slice(fire_w2, (0, rank * heads), (hidden, heads))
-
+    stat_rows = 2 * (-(-heads_count // 8) * 8)
+
+    anywhere = pl.BlockSpec(memory_space=pl.ANY)
     vmem = pl.BlockSpec(memory_space=pltpu.VMEM)
     smem = pl.BlockSpec(memory_space=pltpu.SMEM)
     low = jnp.bfloat16
+    wide = jnp.float32
     block = jax.ShapeDtypeStruct((rows_dev, feature_count), low)
     steps = parts - 1
     dma = pltpu.SemaphoreType.DMA
     grad_q, grad_k, grad_v, sums = pl.pallas_call(
         exchange_kernel,
-        out_shape=(
-            block,
-            block,
-            block,
-            jax.ShapeDtypeStruct((2, heads, hidden, 128), jnp.float32),
-        ),
-        in_specs=[vmem] * 7 + [smem] * 3,
+        out_shape=(block, block, block, jax.ShapeDtypeStruct((hidden, 128), wide)),
+        in_specs=[anywhere] * 5 + [vmem] + [smem] * 4,
         out_specs=(vmem,) * 4,
         scratch_shapes=[
             pltpu.VMEM((4, heads, tokens, head_size), low),
-            pltpu.VMEM((parts, 16, rows_dev), jnp.float32),
-            pltpu.VMEM((heads, tokens, tokens), jnp.float32),
-            pltpu.VMEM((tokens, tokens), jnp.float32),
+            pltpu.VMEM((rows_dev, feature_count), low),
+            pltpu.VMEM((rows_dev, feature_count), low),
+            pltpu.VMEM((rows_dev, 128), wide),
+            pltpu.VMEM((parts, stat_rows, rows_dev), wide),
+            pltpu.VMEM((heads, tokens, tokens), wide),
+            pltpu.VMEM((tokens, tokens), wide),
             pltpu.VMEM((3, heads, tokens, head_size), low),
-            pltpu.VMEM((2, heads, hidden, 8, 128), jnp.float32),
+            pltpu.VMEM((2, heads, hidden, 8, 128), wide),
+            pltpu.VMEM((heads + 2, hidden, 128), wide),
+            pltpu.VMEM((cp_count, hidden, 128), wide),
+            pltpu.VMEM((dp_count, hidden, 128), wide),
+            dma((4, heads)),
+            dma((2,)),
             dma((4, heads, steps)),
             dma((4, heads, steps)),
             dma((steps,)),
             dma((steps,)),
             dma((3, heads, steps)),
             dma((3, heads, steps)),
+            dma((cp_count - 1,)),
+            dma((cp_count - 1,)),
+            dma((dp_count - 1,)),
+            dma((dp_count - 1,)),
         ],
         compiler_params=pltpu.CompilerParams(
             collective_id=0, has_side_effects=True, vmem_limit_bytes=48 * 2**20
         ),
-    )(queries[0], keys[0], values[0], d_out[0], stat, start, rden, fire_w1, fire_b1, w2_mine)
-    sums = jnp.sum(sums, axis=3)
-    flat, tilted = sums[0].T, sums[1].T
-    second = jnp.zeros((hidden, heads_count), jnp.float32)
-    second = lax.dynamic_update_slice(
-        second, fire_w1[:, None] * tilted + fire_b1[:, None] * flat, (0, rank * heads)
-    )
-    first = jnp.sum(w2_mine * tilted, axis=1)
-    bias_sum = jnp.sum(w2_mine * flat, axis=1)
-    joined = jnp.concatenate([second, first[:, None], bias_sum[:, None]], axis=1)
-    factor = (lax.axis_size("dp") * cp_count * rows_dev) ** (-0.5)
-    joined = lax.psum(joined, ("cp", "dp")) * factor
+    )(
+        queries[0],
+        keys[0],
+        values[0],
+        d_out[0],
+        outputs[0],
+        log_norm[0],
+        lengths,
+        fire_w1,
+        fire_b1,
+        fire_w2,
+    )
     return (
         grad_q[None],
         grad_k[None],
         grad_v[None],
-        joined[:, heads_count],
-        joined[:, heads_count + 1],
-        joined[:, :heads_count],
+        sums[:, heads_count],
+        sums[:, heads_count + 1],
+        sums[:, :heads_count],
     )
 
 

time: 110 us -> 78.1 us (0.71)
  blocking collectives: 40.7 us -> 0 us
  Pallas kernels: 57.2 us -> 66.2 us
  other arithmetic: 2.18 us -> 0 us
  local copies, waits for them, and re-layouts: 9.06 us -> 10.9 us
    psum x1 -> x0, blocking collectives: 40.7 us -> none  [by_heads(): joined = lax.psum(joined, ('cp', 'dp')) * factor]
    pallas_call x1, Pallas kernels: 57.2 us -> 66.2 us  [by_heads(): pl.pallas_call(exchange_kernel, out_shape=(block, block, block, jax.Shape...]
    unnamed x27 -> x24, local copies, waits for them, and re-layouts: 8.29 us -> 10.2 us
where the time goes in v2:
time: 78.1 us; the launch traced here: 77.7 us
  Pallas kernels  66.2 us (85%)
  local copies, waits for them, and re-layouts  10.9 us (14%)
    pallas_call x1, Pallas kernels, by_heads(): pl.pallas_call(exchange_kernel, out_shape=(block, block, block, jax.Shape...  66.2 us
    unnamed x24, local copies, waits for them, and re-layouts  10.2 us

profile of v2, /device:TPU:0, one launch (start us, length us, event | category | flops | bytes accessed | tf_op | source)
XLA Modules:
  0.0 77.7 jit_solution(7079751445168052050)
XLA Ops:
  0.6 0.0 copy-start.8
  0.6 0.8 %copy.19 = f32[1,128,20]{2,1,0:T(8,128)S(1)} copy(f32[1,128,20]{1,0,2:T(1,128)} %param.15) | data formatting | bytes 20480 | tf_op args[5]
  1.5 0.0 copy-done.8
  1.5 0.1 copy.20.w2_ref
  1.5 0.0 copy-start.5
  1.5 0.0 copy-start.6
  1.5 0.0 copy-start.7
  1.5 0.6 copy-done.5
  2.2 0.0 copy-done.6
  2.2 0.0 copy-done.7
  2.2 0.0 copy-start
  2.2 1.1 %copy-done = bf16[1,128,2560]{2,1,0:T(8,128)(2,1)S(1)} copy-done((bf16[1,128,2560]{2,1,0:T(8,128)(2,1)S(1)}, bf16[1,128,2560]{2,1,0:T(8,128)(2,1)}, u32[]{:S(2)}) %copy-start) | copy-done | bytes 655384
  3.3 0.0 copy-start.1
  3.3 1.1 %copy-done.1 = bf16[1,128,2560]{2,1,0:T(8,128)(2,1)S(1)} copy-done((bf16[1,128,2560]{2,1,0:T(8,128)(2,1)S(1)}, bf16[1,128,2560]{2,1,0:T(8,128)(2,1)}, u32[]{:S(2)}) %copy-start.1) | copy-done | bytes 655384
  4.4 0.0 copy-start.2
  4.4 1.1 %copy-done.2 = bf16[1,128,2560]{2,1,0:T(8,128)(2,1)S(1)} copy-done((bf16[1,128,2560]{2,1,0:T(8,128)(2,1)S(1)}, bf16[1,128,2560]{2,1,0:T(8,128)(2,1)}, u32[]{:S(2)}) %copy-start.2) | copy-done | bytes 655384
  5.5 0.0 copy-start.3
  5.5 1.1 %copy-done.3 = bf16[1,128,2560]{2,1,0:T(8,128)(2,1)S(1)} copy-done((bf16[1,128,2560]{2,1,0:T(8,128)(2,1)S(1)}, bf16[1,128,2560]{2,1,0:T(8,128)(2,1)}, u32[]{:S(2)}) %copy-start.3) | copy-done | bytes 655384
  6.6 0.0 copy-start.4
  6.6 1.1 %copy-done.4 = bf16[1,128,2560]{2,1,0:T(8,128)(2,1)S(1)} copy-done((bf16[1,128,2560]{2,1,0:T(8,128)(2,1)S(1)}, bf16[1,128,2560]{2,1,0:T(8,128)(2,1)}, u32[]{:S(2)}) %copy-start.4) | copy-done | bytes 655384
  7.7 66.2 %shard_map.145 = (bf16[128,2560]{1,0:T(8,128)(2,1)S(1)}, bf16[128,2560]{1,0:T(8,128)(2,1)S(1)}, bf16[128,2560]{1,0:T(8,128)(2,1)S(1)}, f32[32,128]{1,0:T(8,128)S(1)}) custom-call(bf16[128,2560]{1,0:T(8,128)(2,1)S(1)} %bitcast.13, bf16[128,2560]{1,0:T(8,128)(2,1)S(1)} %bitcast.14, bf16[128,2560]{1,0:T(8,128)(2,1)S(1)} %bitcast.15, ...), custom_call_target="tpu_custom_call" | custom-call | tf_op jit(solution)/shard_map/pallas_call | solution.py:466
  73.8 0.7 slice_reduce_fusion
  74.5 0.7 copy.21
  75.2 0.8 %copy.25 = bf16[1,128,2560]{2,1,0:T(8,128)(2,1)} copy(bf16[1,128,2560]{2,1,0:T(8,128)(2,1)S(1)} %bitcast.12) | data formatting | bytes 1310720
  76.1 0.8 %copy.26 = bf16[1,128,2560]{2,1,0:T(8,128)(2,1)} copy(bf16[1,128,2560]{2,1,0:T(8,128)(2,1)S(1)} %bitcast.11) | data formatting | bytes 1310720
  76.9 0.8 %copy.27 = bf16[1,128,2560]{2,1,0:T(8,128)(2,1)} copy(bf16[1,128,2560]{2,1,0:T(8,128)(2,1)S(1)} %bitcast.10) | data formatting | bytes 1310720
Async XLA Ops:
  0.6 0.8 %copy-start.8 = (f32[32,20]{0,1:T(8,128)S(1)}, f32[32,20]{0,1:T(8,128)}, u32[]{:S(2)}) copy-start(f32[32,20]{0,1:T(8,128)} %param.19) | copy-start | bytes 7684
  1.5 0.7 copy-start.5
  1.5 0.7 copy-start.6
  1.5 0.7 copy-start.7
  2.2 1.1 %copy-start = (bf16[1,128,2560]{2,1,0:T(8,128)(2,1)S(1)}, bf16[1,128,2560]{2,1,0:T(8,128)(2,1)}, u32[]{:S(2)}) copy-start(bf16[1,128,2560]{2,1,0:T(8,128)(2,1)} %param.10) | copy-start | bytes 1966084
  3.3 1.1 %copy-start.1 = (bf16[1,128,2560]{2,1,0:T(8,128)(2,1)S(1)}, bf16[1,128,2560]{2,1,0:T(8,128)(2,1)}, u32[]{:S(2)}) copy-start(bf16[1,128,2560]{2,1,0:T(8,128)(2,1)} %param.11) | copy-start | bytes 1966084
  4.4 1.1 %copy-start.2 = (bf16[1,128,2560]{2,1,0:T(8,128)(2,1)S(1)}, bf16[1,128,2560]{2,1,0:T(8,128)(2,1)}, u32[]{:S(2)}) copy-start(bf16[1,128,2560]{2,1,0:T(8,128)(2,1)} %param.12) | copy-start | bytes 1966084
  5.5 1.1 %copy-start.3 = (bf16[1,128,2560]{2,1,0:T(8,128)(2,1)S(1)}, bf16[1,128,2560]{2,1,0:T(8,128)(2,1)}, u32[]{:S(2)}) copy-start(bf16[1,128,2560]{2,1,0:T(8,128)(2,1)} %param.14) | copy-start | bytes 1966084
  6.6 1.1 %copy-start.4 = (bf16[1,128,2560]{2,1,0:T(8,128)(2,1)S(1)}, bf16[1,128,2560]{2,1,0:T(8,128)(2,1)}, u32[]{:S(2)}) copy-start(bf16[1,128,2560]{2,1,0:T(8,128)(2,1)} %param.13) | copy-start | bytes 1966084

commit v3 on v2

--- a/solution.py
+++ b/solution.py
@@ -94,8 +94,9 @@
 NN = (((1,), (0,)), ((), ()))
 TN = (((0,), (0,)), ((), ()))
 MASKED = -1e30
+VMEM_BYTES = 62 * 2**20
 BIAS_ROWS = 32
-SUM_ROWS = 32
+SUM_ROWS = 64
 
 
 def exchange_kernel(
@@ -112,17 +113,17 @@
     dq_ref,
     dk_ref,
     dv_ref,
-    sums_ref,
+    second_ref,
+    lines_ref,
     held,
     own_g,
     own_o,
-    padded,
     stats,
     pair,
     ratios,
     grads,
     acc,
-    lanes,
+    coefs,
     cp_slots,
     dp_slots,
     own_sem,
@@ -253,10 +254,8 @@
     early = 2
     lax.fori_loop(0, early, send_head, 0)
 
-    padded[...] = jnp.zeros_like(padded)
-    padded[:, 0:heads_count] = log_ref[...]
     stats[rank] = jnp.zeros(stats.shape[1:], jnp.float32)
-    stats[rank, 0:delta_at, :] = padded[...].T[0:delta_at]
+    stats[rank, 0:heads_count, :] = log_ref[:, 0, :]
     for copy in delta_copies:
         copy.wait()
     ones = jnp.ones((8, 2 * size), jnp.bfloat16)
@@ -299,7 +298,7 @@
             for unit in range(hidden):
                 act = jnp.maximum(ratio * w1_ref[unit] + b1_ref[unit], 0.0)
                 for head in range(heads):
-                    totals[head] = totals[head] + act * w2_ref[unit, rank * heads + head]
+                    totals[head] = totals[head] + act * w2_ref[rank * heads + head, unit]
             for head in range(heads):
                 pair[head, at, columns] = jnp.where(allowed, totals[head], MASKED)
             return carry
@@ -314,6 +313,15 @@
                 jnp.full((rows, rows), MASKED, jnp.float32)
             )
     acc[...] = jnp.zeros_like(acc)
+    unit_at = lax.broadcasted_iota(jnp.int32, (hidden, 128), 0)
+    lane_at = lax.broadcasted_iota(jnp.int32, (hidden, 128), 1)
+    coef = jnp.zeros((hidden, 128), jnp.float32)
+    for unit in range(hidden):
+        line = jnp.where(lane_at == 0, w1_ref[unit], b1_ref[unit])
+        for head in range(heads):
+            line = jnp.where(lane_at == 2 + head, w2_ref[rank * heads + head, unit], line)
+        coef = jnp.where(unit_at == unit, line, coef)
+    coefs[...] = coef
 
     for step in range(1, parts):
         stat_copy(step).wait_recv()
@@ -365,53 +373,58 @@
             results[array][:, head_columns(rank, head)] = grads[array, head, row_block(rank), :]
         return carry
 
-    def sum_heads(some):
-        def sum_column(block, carry):
-            columns = row_block(block)
-
-            def sum_rows(chunk, carry):
-                at = pl.ds(pl.multiple_of(chunk * SUM_ROWS, SUM_ROWS), SUM_ROWS)
-                ratio = ratios[at, columns]
-                flat = {head: pair[head, at, columns] for head in some}
-                tilted = {head: flat[head] * ratio for head in some}
-                for unit in range(hidden):
-                    live = ratio * w1_ref[unit] > -b1_ref[unit]
-                    for head in some:
-                        for kind, term in ((0, flat[head]), (1, tilted[head])):
-                            kept = jnp.where(live, term, 0.0)
-                            part = kept[0:8]
-                            for row in range(8, SUM_ROWS, 8):
-                                part = part + kept[row : row + 8]
-                            acc[kind, head, unit] += part
-                return carry
-
-            return lax.fori_loop(0, (block + 1) * (rows // SUM_ROWS), sum_rows, carry)
-
-        lax.fori_loop(0, parts, sum_column, 0)
-
-    lax.fori_loop(0, early, one_head, 0)
-    sum_heads(range(0, early))
-    lax.fori_loop(early, heads, one_head, 0)
-    sum_heads(range(early, heads))
-
-    for unit in range(hidden):
-        first = jnp.zeros((8, 128), jnp.float32)
-        bias_sum = jnp.zeros((8, 128), jnp.float32)
-        for head in range(heads):
-            flat, tilted = acc[0, head, unit], acc[1, head, unit]
-            weight = w2_ref[unit, rank * heads + head]
-            first = first + tilted * weight
-            bias_sum = bias_sum + flat * weight
-            second = tilted * w1_ref[unit] + flat * b1_ref[unit]
-            lanes[head, unit : unit + 1, :] = jnp.sum(second, axis=0, keepdims=True)
-        lanes[heads, unit : unit + 1, :] = jnp.sum(first, axis=0, keepdims=True)
-        lanes[heads + 1, unit : unit + 1, :] = jnp.sum(bias_sum, axis=0, keepdims=True)
+    lax.fori_loop(0, heads, one_head, 0)
+
+    def sum_column(block, carry):
+        columns = row_block(block)
+
+        def sum_rows(chunk, carry):
+            at = pl.ds(pl.multiple_of(chunk * SUM_ROWS, SUM_ROWS), SUM_ROWS)
+            ratio = ratios[at, columns]
+            flat = [pair[head, at, columns] for head in range(heads)]
+            lives, terms = [], []
+            for row in range(0, SUM_ROWS, 8):
+                part = ratio[row : row + 8]
+                live = [
+                    jnp.where(part * w1_ref[unit] > -b1_ref[unit], 1.0, 0.0)
+                    for unit in range(hidden)
+                ]
+                lives.append(jnp.concatenate(live, axis=0).astype(jnp.bfloat16))
+                term = [flat[head][row : row + 8] for head in range(heads)]
+                term = jnp.concatenate(term + [one * part for one in term], axis=0)
+                high = term.astype(jnp.bfloat16)
+                rest = (term - high.astype(jnp.float32)).astype(jnp.bfloat16)
+                terms.append(jnp.concatenate([high, rest], axis=0))
+            acc[...] += dot(
+                jnp.concatenate(lives, axis=1), jnp.concatenate(terms, axis=1), NT
+            )
+            return carry
+
+        return lax.fori_loop(0, (block + 1) * (rows // SUM_ROWS), sum_rows, carry)
+
+    lax.fori_loop(0, parts, sum_column, 0)
+
+    across = acc.shape[1]
+    same = lax.rem(lax.broadcasted_iota(jnp.int32, acc.shape, 0), 8) == lax.rem(
+        lax.broadcasted_iota(jnp.int32, acc.shape, 1), 8
+    )
+    folded = jnp.sum(jnp.where(same, acc[...], 0.0).reshape(hidden, 8, across), axis=1)
+    kind = lax.rem(lax.broadcasted_iota(jnp.int32, (hidden, across), 1) // 8, 2 * heads)
     lane = lax.broadcasted_iota(jnp.int32, (hidden, 128), 1)
     message = jnp.zeros((hidden, 128), jnp.float32)
-    for index in range(heads + 2):
-        place = rank * heads + index if index < heads else heads_count + index - heads
-        column = jnp.sum(lanes[index], axis=1, keepdims=True)
-        message = jnp.where(lane == place, column, message)
+    first = jnp.zeros((hidden, 1), jnp.float32)
+    bias_sum = jnp.zeros((hidden, 1), jnp.float32)
+    w1_column, b1_column = coefs[:, 0:1], coefs[:, 1:2]
+    for head in range(heads):
+        flat = jnp.sum(jnp.where(kind == head, folded, 0.0), axis=1, keepdims=True)
+        tilted = jnp.sum(jnp.where(kind == heads + head, folded, 0.0), axis=1, keepdims=True)
+        weight = coefs[:, 2 + head : 3 + head]
+        first = first + tilted * weight
+        bias_sum = bias_sum + flat * weight
+        second = tilted * w1_column + flat * b1_column
+        message = jnp.where(lane == rank * heads + head, second, message)
+    message = jnp.where(lane == heads_count, first, message)
+    message = jnp.where(lane == heads_count + 1, bias_sum, message)
     cp_slots[me] = message
     for step in range(1, cp_count):
         cp_copy(step).start()
@@ -428,7 +441,9 @@
     total = dp_slots[0]
     for index in range(1, dp_count):
         total = total + dp_slots[index]
-    sums_ref[...] = total * (dp_count * cp_count * rows) ** (-0.5)
+    total = (total * (dp_count * cp_count * rows) ** (-0.5)).T
+    second_ref[...] = total[0:heads_count]
+    lines_ref[...] = total[heads_count : heads_count + 2]
 
     def drain_head(head, carry):
         for step in (2, 1, 3):
@@ -455,7 +470,7 @@
     tokens = parts * rows_dev
     stat_rows = 2 * (-(-heads_count // 8) * 8)
 
-    anywhere = pl.BlockSpec(memory_space=pl.ANY)
+    hbm = pl.BlockSpec(memory_space=pltpu.HBM)
     vmem = pl.BlockSpec(memory_space=pltpu.VMEM)
     smem = pl.BlockSpec(memory_space=pltpu.SMEM)
     low = jnp.bfloat16
@@ -463,22 +478,27 @@
     block = jax.ShapeDtypeStruct((rows_dev, feature_count), low)
     steps = parts - 1
     dma = pltpu.SemaphoreType.DMA
-    grad_q, grad_k, grad_v, sums = pl.pallas_call(
+    grad_q, grad_k, grad_v, second, lines = pl.pallas_call(
         exchange_kernel,
-        out_shape=(block, block, block, jax.ShapeDtypeStruct((hidden, 128), wide)),
-        in_specs=[anywhere] * 5 + [vmem] + [smem] * 4,
-        out_specs=(vmem,) * 4,
+        out_shape=(
+            block,
+            block,
+            block,
+            jax.ShapeDtypeStruct((heads_count, hidden), wide),
+            jax.ShapeDtypeStruct((2, hidden), wide),
+        ),
+        in_specs=[hbm] * 5 + [vmem] + [smem] * 4,
+        out_specs=(vmem,) * 5,
         scratch_shapes=[
             pltpu.VMEM((4, heads, tokens, head_size), low),
             pltpu.VMEM((rows_dev, feature_count), low),
             pltpu.VMEM((rows_dev, feature_count), low),
-            pltpu.VMEM((rows_dev, 128), wide),
             pltpu.VMEM((parts, stat_rows, rows_dev), wide),
             pltpu.VMEM((heads, tokens, tokens), wide),
             pltpu.VMEM((tokens, tokens), wide),
             pltpu.VMEM((3, heads, tokens, head_size), low),
-            pltpu.VMEM((2, heads, hidden, 8, 128), wide),
-            pltpu.VMEM((heads + 2, hidden, 128), wide),
+            pltpu.VMEM((hidden * 8, 4 * heads * 8), wide),
+            pltpu.VMEM((hidden, 128), wide),
             pltpu.VMEM((cp_count, hidden, 128), wide),
             pltpu.VMEM((dp_count, hidden, 128), wide),
             dma((4, heads)),
@@ -495,7 +515,7 @@
             dma((dp_count - 1,)),
         ],
         compiler_params=pltpu.CompilerParams(
-            collective_id=0, has_side_effects=True, vmem_limit_bytes=48 * 2**20
+            collective_id=0, has_side_effects=True, vmem_limit_bytes=VMEM_BYTES
         ),
     )(
         queries[0],
@@ -503,19 +523,19 @@
         values[0],
         d_out[0],
         outputs[0],
-        log_norm[0],
+        log_norm.transpose(2, 0, 1),
         lengths,
         fire_w1,
         fire_b1,
-        fire_w2,
+        fire_w2.T,
     )
     return (
         grad_q[None],
         grad_k[None],
         grad_v[None],
-        sums[:, heads_count],
-        sums[:, heads_count + 1],
-        sums[:, :heads_count],
+        lines[0],
+        lines[1],
+        second.T,
     )
 
 

time: 78.1 us -> 74.5 us (0.954)
  local copies, waits for them, and re-layouts: 10.9 us -> 5.98 us
  Pallas kernels: 66.2 us -> 67.6 us
    unnamed x24 -> x12, local copies, waits for them, and re-layouts: 10.2 us -> 5.46 us
    pallas_call x1, Pallas kernels: 66.2 us -> 67.6 us  [by_heads(): pl.pallas_call(exchange_kernel, out_shape=(block, block, block, jax.Shape...]
where the time goes in v3:
time: 74.5 us; the launch traced here: 74.2 us
  Pallas kernels  67.6 us (91%)
  local copies, waits for them, and re-layouts  5.98 us (8%)
    pallas_call x1, Pallas kernels, by_heads(): pl.pallas_call(exchange_kernel, out_shape=(block, block, block, jax.Shape...  67.6 us
    unnamed x12, local copies, waits for them, and re-layouts  5.46 us

profile of v3, /device:TPU:0, one launch (start us, length us, event | category | flops | bytes accessed | tf_op | source)
XLA Modules:
  0.0 74.2 jit_solution(4803035294883239653)
XLA Ops:
  0.6 67.6 %shard_map.145 = (bf16[128,2560]{1,0:T(8,128)(2,1)}, bf16[128,2560]{1,0:T(8,128)(2,1)}, bf16[128,2560]{1,0:T(8,128)(2,1)}, f32[20,32]{1,0:T(8,128)}, f32[2,32]{1,0:T(2,128)}) custom-call(bf16[128,2560]{1,0:T(8,128)(2,1)} %bitcast.18, bf16[128,2560]{1,0:T(8,128)(2,1)} %bitcast.19, bf16[128,2560]{1,0:T(8,128)(2,1)} %bitcast.20, bf16[128,2560]{1,0:T(8,128)(2,1)} %bitcast.21, ...), custom_call_target="tpu_custom_call" | custom-call | tf_op jit(solution)/shard_map/pallas_call | solution.py:481
  68.2 0.0 copy-start.3
  68.2 0.7 copy-done.3
  68.9 0.5 slice_bitcast_fusion
  69.4 0.0 copy-start.1
  69.4 2.0 %copy.20 = bf16[1,128,2560]{2,1,0:T(8,128)(2,1)} copy(bf16[1,128,2560]{2,1,0:T(8,128)(2,1)} %bitcast.17) | data formatting | bytes 1310720
  71.4 0.0 copy-done.1
  71.4 0.0 copy-start
  71.4 0.8 %copy.21 = bf16[1,128,2560]{2,1,0:T(8,128)(2,1)} copy(bf16[1,128,2560]{2,1,0:T(8,128)(2,1)S(1)} %bitcast.16) | data formatting | bytes 1310720
  72.3 0.5 copy-done
  72.8 0.0 copy-start.2
  72.8 0.8 %copy.22 = bf16[1,128,2560]{2,1,0:T(8,128)(2,1)} copy(bf16[1,128,2560]{2,1,0:T(8,128)(2,1)S(1)} %bitcast.15) | data formatting | bytes 1310720
  73.6 0.0 copy-done.2
  73.6 0.6 copy.23
Async XLA Ops:
  68.2 0.7 copy-start.3
  69.4 2.0 %copy-start.1 = (bf16[128,2560]{1,0:T(8,128)(2,1)S(1)}, bf16[128,2560]{1,0:T(8,128)(2,1)}, u32[]{:S(2)}) copy-start(bf16[128,2560]{1,0:T(8,128)(2,1)} %get-tuple-element.12) | copy-start | bytes 1966084
  71.4 1.3 %copy-start = (bf16[128,2560]{1,0:T(8,128)(2,1)S(1)}, bf16[128,2560]{1,0:T(8,128)(2,1)}, u32[]{:S(2)}) copy-start(bf16[128,2560]{1,0:T(8,128)(2,1)} %get-tuple-element.13) | copy-start | bytes 1966084
  72.8 0.8 %copy-start.2 = (f32[20,32]{1,0:T(8,128)S(1)}, f32[20,32]{1,0:T(8,128)}, u32[]{:S(2)}) copy-start(f32[20,32]{1,0:T(8,128)} %get-tuple-element.15) | copy-start | bytes 7684

commit v4 on v3

--- a/solution.py
+++ b/solution.py
@@ -366,14 +366,19 @@
             grads[0, head, trows, :] = (dq[tile] * scale_value).astype(jnp.bfloat16)
             grads[1, head, trows, :] = (dk[tile] * scale_value).astype(jnp.bfloat16)
             grads[2, head, trows, :] = dv[tile].astype(jnp.bfloat16)
+        for array in range(3):
+            results[array][:, head_columns(rank, head)] = grads[array, head, row_block(rank), :]
+        return carry
+
+    def return_head(head, carry):
         for step in (2, 1, 3):
             for array in range(3):
                 out_copy(array, head, step).start()
-        for array in range(3):
-            results[array][:, head_columns(rank, head)] = grads[array, head, row_block(rank), :]
         return carry
 
-    lax.fori_loop(0, heads, one_head, 0)
+    prompt = heads - 2
+    lax.fori_loop(0, prompt, lambda head, carry: return_head(head, one_head(head, carry)), 0)
+    lax.fori_loop(prompt, heads, one_head, 0)
 
     def sum_column(block, carry):
         columns = row_block(block)
@@ -428,6 +433,7 @@
     cp_slots[me] = message
     for step in range(1, cp_count):
         cp_copy(step).start()
+    lax.fori_loop(prompt, heads, return_head, 0)
     for step in range(1, cp_count):
         cp_copy(step).wait()
     total = cp_slots[0]

time: 74.5 us -> 71.2 us (0.956)
  Pallas kernels: 67.6 us -> 64.2 us
    pallas_call x1, Pallas kernels: 67.6 us -> 64.2 us  [by_heads(): pl.pallas_call(exchange_kernel, out_shape=(block, block, block, jax.Shape...]
where the time goes in v4:
time: 71.2 us; the launch traced here: 70.9 us
  Pallas kernels  64.2 us (90%)
  local copies, waits for them, and re-layouts  5.98 us (8%)
    pallas_call x1, Pallas kernels, by_heads(): pl.pallas_call(exchange_kernel, out_shape=(block, block, block, jax.Shape...  64.2 us
    unnamed x12, local copies, waits for them, and re-layouts  5.46 us

profile of v4, /device:TPU:0, one launch (start us, length us, event | category | flops | bytes accessed | tf_op | source)
XLA Modules:
  0.0 70.9 jit_solution(9713473706677990292)
XLA Ops:
  0.6 64.2 %shard_map.145 = (bf16[128,2560]{1,0:T(8,128)(2,1)}, bf16[128,2560]{1,0:T(8,128)(2,1)}, bf16[128,2560]{1,0:T(8,128)(2,1)}, f32[20,32]{1,0:T(8,128)}, f32[2,32]{1,0:T(2,128)}) custom-call(bf16[128,2560]{1,0:T(8,128)(2,1)} %bitcast.18, bf16[128,2560]{1,0:T(8,128)(2,1)} %bitcast.19, bf16[128,2560]{1,0:T(8,128)(2,1)} %bitcast.20, bf16[128,2560]{1,0:T(8,128)(2,1)} %bitcast.21, ...), custom_call_target="tpu_custom_call" | custom-call | tf_op jit(solution)/shard_map/pallas_call | solution.py:487
  64.9 0.0 copy-start.3
  64.9 0.7 copy-done.3
  65.6 0.5 slice_bitcast_fusion
  66.1 0.0 copy-start.1
  66.1 2.0 %copy.20 = bf16[1,128,2560]{2,1,0:T(8,128)(2,1)} copy(bf16[1,128,2560]{2,1,0:T(8,128)(2,1)} %bitcast.17) | data formatting | bytes 1310720
  68.1 0.0 copy-done.1
  68.1 0.0 copy-start
  68.1 0.8 %copy.21 = bf16[1,128,2560]{2,1,0:T(8,128)(2,1)} copy(bf16[1,128,2560]{2,1,0:T(8,128)(2,1)S(1)} %bitcast.16) | data formatting | bytes 1310720
  69.0 0.5 copy-done
  69.4 0.0 copy-start.2
  69.4 0.8 %copy.22 = bf16[1,128,2560]{2,1,0:T(8,128)(2,1)} copy(bf16[1,128,2560]{2,1,0:T(8,128)(2,1)S(1)} %bitcast.15) | data formatting | bytes 1310720
  70.3 0.0 copy-done.2
  70.3 0.6 copy.23
Async XLA Ops:
  64.9 0.7 copy-start.3
  66.1 2.0 %copy-start.1 = (bf16[128,2560]{1,0:T(8,128)(2,1)S(1)}, bf16[128,2560]{1,0:T(8,128)(2,1)}, u32[]{:S(2)}) copy-start(bf16[128,2560]{1,0:T(8,128)(2,1)} %get-tuple-element.12) | copy-start | bytes 1966084
  68.1 1.3 %copy-start = (bf16[128,2560]{1,0:T(8,128)(2,1)S(1)}, bf16[128,2560]{1,0:T(8,128)(2,1)}, u32[]{:S(2)}) copy-start(bf16[128,2560]{1,0:T(8,128)(2,1)} %get-tuple-element.13) | copy-start | bytes 1966084
  69.4 0.8 %copy-start.2 = (f32[20,32]{1,0:T(8,128)S(1)}, f32[20,32]{1,0:T(8,128)}, u32[]{:S(2)}) copy-start(f32[20,32]{1,0:T(8,128)} %get-tuple-element.15) | copy-start | bytes 7684

commit v5 on v4

--- a/solution.py
+++ b/solution.py
@@ -110,9 +110,7 @@
     w1_ref,
     b1_ref,
     w2_ref,
-    dq_ref,
-    dk_ref,
-    dv_ref,
+    grad_ref,
     second_ref,
     lines_ref,
     held,
@@ -152,7 +150,7 @@
     rank = lax.rem(me, parts)
     base = me - rank
     inputs = (q_ref, k_ref, v_ref, g_ref)
-    results = (dq_ref, dk_ref, dv_ref)
+    results = tuple(grad_ref.at[array] for array in range(3))
 
     def dot(a, b, dims):
         return lax.dot_general(a, b, dims, preferred_element_type=jnp.float32)
@@ -481,20 +479,18 @@
     smem = pl.BlockSpec(memory_space=pltpu.SMEM)
     low = jnp.bfloat16
     wide = jnp.float32
-    block = jax.ShapeDtypeStruct((rows_dev, feature_count), low)
+    block = jax.ShapeDtypeStruct((3, rows_dev, feature_count), low)
     steps = parts - 1
     dma = pltpu.SemaphoreType.DMA
-    grad_q, grad_k, grad_v, second, lines = pl.pallas_call(
+    joined, second, lines = pl.pallas_call(
         exchange_kernel,
         out_shape=(
-            block,
-            block,
             block,
             jax.ShapeDtypeStruct((heads_count, hidden), wide),
             jax.ShapeDtypeStruct((2, hidden), wide),
         ),
         in_specs=[hbm] * 5 + [vmem] + [smem] * 4,
-        out_specs=(vmem,) * 5,
+        out_specs=(vmem,) * 3,
         scratch_shapes=[
             pltpu.VMEM((4, heads, tokens, head_size), low),
             pltpu.VMEM((rows_dev, feature_count), low),
@@ -536,9 +532,9 @@
         fire_w2.T,
     )
     return (
-        grad_q[None],
-        grad_k[None],
-        grad_v[None],
+        joined[0:1],
+        joined[1:2],
+        joined[2:3],
         lines[0],
         lines[1],
         second.T,

time: 71.2 us -> 69 us (0.969)
  local copies, waits for them, and re-layouts: 5.98 us -> 3.92 us
    unnamed x12 -> x5, local copies, waits for them, and re-layouts: 5.46 us -> 0.61 us
    slice x0 -> x1, local copies, waits for them, and re-layouts: none -> 2.8 us  [by_heads(): return (joined[0:1], joined[1:2], joined[2:3], lines[0], lines[1], second.T)]
where the time goes in v5:
time: 69 us; the launch traced here: 68.8 us
  Pallas kernels  64.2 us (93%)
  local copies, waits for them, and re-layouts  3.92 us (6%)
    pallas_call x1, Pallas kernels, by_heads(): pl.pallas_call(exchange_kernel, out_shape=(block, jax.ShapeDtypeStruct((h...  64.2 us
    slice x1, local copies, waits for them, and re-layouts, by_heads(): return (joined[0:1], joined[1:2], joined[2:3], lines[0], lines[1], second.T)  2.8 us

profile of v5, /device:TPU:0, one launch (start us, length us, event | category | flops | bytes accessed | tf_op | source)
XLA Modules:
  0.0 68.8 jit_solution(10622260826124090150)
XLA Ops:
  0.6 64.2 %shard_map.145 = (bf16[3,128,2560]{2,1,0:T(8,128)(2,1)}, f32[20,32]{1,0:T(8,128)}, f32[2,32]{1,0:T(2,128)}) custom-call(bf16[128,2560]{1,0:T(8,128)(2,1)} %bitcast.12, bf16[128,2560]{1,0:T(8,128)(2,1)} %bitcast.13, bf16[128,2560]{1,0:T(8,128)(2,1)} %bitcast.14, bf16[128,2560]{1,0:T(8,128)(2,1)} %bitcast.15, bf16[128,2560]{1,0:T(8,128)(2,1)} %bitcast.16, ...), custom_call_target="tpu_custom_call" | custom-call | tf_op jit(solution)/shard_map/pallas_call | solution.py:485
  64.9 0.0 copy-start.1
  64.9 0.0 copy-start
  64.9 2.8 %fusion = (bf16[1,128,2560]{2,1,0:T(8,128)(2,1)}, bf16[1,128,2560]{2,1,0:T(8,128)(2,1)}, bf16[1,128,2560]{2,1,0:T(8,128)(2,1)}) fusion(bf16[3,128,2560]{2,1,0:T(8,128)(2,1)} %get-tuple-element.9), kind=kLoop, calls=%fused_computation.2 | loop fusion | bytes 3932160 | tf_op jit(solution)/shard_map/slice | solution.py:537
  67.7 0.0 copy-done.1
  67.7 0.5 slice_bitcast_fusion
  68.2 0.0 copy-done
  68.2 0.6 copy.17
Async XLA Ops:
  64.9 2.8 %copy-start.1 = (f32[2,32]{1,0:T(2,128)S(1)}, f32[2,32]{1,0:T(2,128)}, u32[]{:S(2)}) copy-start(f32[2,32]{1,0:T(2,128)} %get-tuple-element.10) | copy-start | bytes 772
  64.9 3.3 %copy-start = (f32[20,32]{1,0:T(8,128)S(1)}, f32[20,32]{1,0:T(8,128)}, u32[]{:S(2)}) copy-start(f32[20,32]{1,0:T(8,128)} %get-tuple-element.11) | copy-start | bytes 7684
